TPU v7x, 32 devices: a whole 2x2x4 slice. The times are simulated.
32 devices in a mesh: row: 8 (over y, x, core), col: 4 (over z).
Axes of the slice: x: 2, y: 2, z: 4, core: 2. Of those that a mesh axis runs over, the one named last changes fastest.
Arguments:
- blocks: float32 [8, 4, 288, 4096], P('row', 'col')
- block_slot: int32 [8, 4, 288], P('row', 'col'), may hold values from 0 to 73727, as said below
- sign_vec: int32 [98304], P(('col', 'row')), may hold values from -1 to 1, as said below
Outputs:
- normed_image: float32 [98304, 64], P(('col', 'row'))
- power_image: float32 [98304, 64], P(('col', 'row'))
Inputs may be any that keep to these rules, and one draw needn't show every extreme that they name: `block_slot`: each entry is i * 192 + j for a local block row i and block column j; the entries of one device are distinct, and each device names slot 0 and the last slot. `sign_vec`: every entry is -1 or 1.
All inputs are finite; a program needn't handle non-finite values.
Results may differ from a plain program's by a relative error of at most 0.0001.
Values sent between devices are 32-bit elements; how exact they have to be, the bound alone decides.
A program may use at most 128 MiB of HBM per device.

v0:
```python
import jax
import jax.numpy as jnp
from jax import lax
from jax.sharding import PartitionSpec as P

BLOCK = 64
PROBES = 64


def hadamard_sign(row_ids, probe_count):
    low_bits = row_ids % 128
    probe_ids = jnp.arange(probe_count, dtype=jnp.int32)
    parity = jnp.zeros((row_ids.shape[0], probe_count), jnp.int32)
    for bit_pos in range(7):
        left_bit = jnp.bitwise_and(jnp.right_shift(low_bits, bit_pos), 1)
        right_bit = jnp.bitwise_and(jnp.right_shift(probe_ids, bit_pos), 1)
        parity = parity + left_bit[:, None] * right_bit[None, :]
    return (1 - 2 * (parity % 2)).astype(jnp.float32)


def block_products(tiles, field, sources, targets, target_count, transpose):
    probe_count = field.shape[1]
    picked = field.reshape(-1, BLOCK, probe_count)[sources]
    pattern_text = "bji,bjk->bik" if transpose else "bij,bjk->bik"
    products = jnp.einsum(pattern_text, tiles, picked, precision=lax.Precision.HIGHEST)
    one_hot = (targets[None, :] == jnp.arange(target_count, dtype=jnp.int32)[:, None]).astype(
        jnp.float32
    )
    summed = jnp.dot(
        one_hot,
        products.reshape(tiles.shape[0], BLOCK * probe_count),
        precision=lax.Precision.HIGHEST,
        preferred_element_type=jnp.float32,
    )
    return summed.reshape(target_count * BLOCK, probe_count)


def local(blocks, block_slot, sign_vec):
    local_rows = sign_vec.shape[0]
    n_rows_axis = lax.axis_size("row")
    n_cols_axis = lax.axis_size("col")
    total_rows = local_rows * n_rows_axis * n_cols_axis
    band_rows = total_rows // n_cols_axis
    row_blocks = band_rows // BLOCK
    col_blocks = total_rows // n_rows_axis // BLOCK
    row_index = lax.axis_index("row")
    col_index = lax.axis_index("col")
    tiles = blocks.reshape(-1, BLOCK, BLOCK)
    slots = block_slot.reshape(-1)
    blk_row = slots // col_blocks
    blk_col = slots % col_blocks
    own_ids = (
        col_index * band_rows + row_index * local_rows + jnp.arange(local_rows, dtype=jnp.int32)
    )
    own_panel = sign_vec.astype(jnp.float32)[:, None] * hadamard_sign(own_ids, PROBES)
    panel = lax.all_gather(own_panel, "col", axis=0, tiled=True)
    partial_value = block_products(tiles, panel, blk_col, blk_row, row_blocks, False)
    first_own = lax.psum_scatter(partial_value, "row", scatter_dimension=0, tiled=True)
    col_sums = lax.psum(jnp.sum(first_own * first_own, axis=0), ("row", "col"))
    normed_own = first_own / jnp.sqrt(col_sums / total_rows + 1e-06)
    normed_col_band = lax.all_gather(normed_own, "row", axis=0, tiled=True)
    second_partial = block_products(tiles, normed_col_band, blk_row, blk_col, col_blocks, True)
    power_own = lax.psum_scatter(second_partial, "col", scatter_dimension=0, tiled=True)
    return (normed_own, power_own)


def solution(mesh):
    in_specs = (P("row", "col", None, None), P("row", "col", None), P(("col", "row")))
    out_specs = (P(("col", "row"), None), P(("col", "row"), None))
    return jax.shard_map(local, mesh=mesh, in_specs=in_specs, out_specs=out_specs, check_vma=False)
```

profile of v0, /device:TPU:0, one launch (start us, length us, event | category | flops | bytes accessed | tf_op | source)
XLA Modules:
  0.0 573.4 jit_solution(14866779846421602721)
XLA Ops:
  7.2 0.0 all-gather.3.cloned.1.call-start
  7.3 0.7 convert_element_type.8
  8.1 4.6 fusion.4
  12.7 0.0 all-gather.3.cloned.1.call-update
  12.7 0.0 reduce-scatter.3.cloned.1.call-start
  12.7 6.2 %copy.7 = f32[1,1,288,4096]{2,3,1,0:T(8,128)} copy(f32[1,1,288,4096]{3,2,1,0:T(8,128)} %param.3) | data formatting | bytes 9437184 | tf_op args[0]
  19.0 12.3 %copy.9 = f32[288,64,64]{2,1,0:T(8,128)} copy(f32[288,64,64]{0,2,1:T(8,128)} %bitcast.32) | data formatting | bytes 9437184 | tf_op jit(solution)/shard_map/reshape | solution.py:48
  31.4 99.5 %all-gather.3.cloned.1.call-done = f32[12288,64]{1,0:T(8,128)} async-done(((f32[3072,64]{1,0:T(8,128)}), f32[12288,64]{1,0:T(8,128)}) %all-gather.3.cloned.1.call-update) | async-done | bytes 3145744 | tf_op jit(solution)/shard_map/all_gather | solution.py:56
  130.9 7.6 %gather_fusion = f32[288,64,64]{2,1,0:T(8,128)} fusion(f32[192,64,64]{2,1,0:T(8,128)} %bitcast.33, s32[1024]{0:T(1024)S(1)} %pad_clamp_fusion.1), kind=kCustom, calls=%fused_computation | custom fusion | bytes 9438336 | tf_op jit(solution)/shard_map/gather | solution.py:23
  138.5 21.5 %convolution_bitcast_fusion.1 = f32[288,64,64]{1,2,0:T(8,128)} fusion(f32[288,64,64]{2,1,0:T(8,128)} %gather_fusion, f32[288,64,64]{2,1,0:T(8,128)} %copy.9), kind=kOutput, calls=%fused_computation.3 | convolution fusion | flops 905969664 | bytes 14155776 | tf_op jit(solution)/shard_map/bij,bjk->bik/dot_general | solution.py:25
  159.9 11.7 %copy.10 = f32[288,64,64]{0,2,1:T(8,128)} copy(f32[288,64,64]{1,2,0:T(8,128)} %convolution_bitcast_fusion.1) | data formatting | bytes 9437184 | tf_op jit(solution)/shard_map/bij,bjk->bik/dot_general | solution.py:25
  171.6 12.3 %fusion.5 = f32[384,4096]{1,0:T(8,128)} fusion(f32[288,4096]{0,1:T(8,128)} %bitcast.31, s32[288]{0:T(512)S(1)} %get-tuple-element.9), kind=kOutput, calls=%fused_computation.15 | convolution fusion | flops 5435928576 | bytes 11011200 | tf_op jit(solution)/shard_map/dot_general | solution.py:29
  183.9 10.8 %reshape.223 = f32[24576,64]{1,0:T(8,128)} reshape(f32[384,4096]{1,0:T(8,128)} %fusion.5) | data formatting | bytes 12582912 | tf_op jit(solution)/shard_map/reshape | solution.py:35
  194.7 0.0 reduce-scatter.3.cloned.1.call-update
  194.7 0.0 all-gather.5.cloned.1.call-start
  194.8 90.7 %reduce-scatter.3.cloned.1.call-done = f32[3072,64]{1,0:T(8,128)} async-done(((f32[24576,64]{1,0:T(8,128)}), f32[3072,64]{1,0:T(8,128)}) %reduce-scatter.3.cloned.1.call-update) | async-done | bytes 786448 | tf_op jit(solution)/shard_map/reduce_scatter | solution.py:58
  285.5 1.9 multiply_reduce_fusion
  287.4 39.3 %psum.7 = f32[64]{0:T(128)S(1)} all-reduce(f32[64]{0:T(128)S(1)} %multiply_reduce_fusion), channel_id=1, replica_groups=mesh['row'=8,'col'=4] {'row','col'}, use_global_device_ids=true, to_apply=%region_2.3 | all-reduce | flops 64 | bytes 512 | tf_op jit(solution)/shard_map/psum | solution.py:59
  326.8 1.3 broadcast_divide_fusion
  328.1 0.0 all-gather.5.cloned.1.call-update
  328.1 0.0 reduce-scatter.5.cloned.1.call-start
  328.2 72.7 %all-gather.5.cloned.1.call-done = f32[24576,64]{1,0:T(8,128)} async-done(((f32[3072,64]{1,0:T(8,128)}), f32[24576,64]{1,0:T(8,128)}) %all-gather.5.cloned.1.call-update) | async-done | bytes 6291472 | tf_op jit(solution)/shard_map/all_gather | solution.py:61
  400.9 9.4 %gather_fusion.1 = f32[288,64,64]{2,1,0:T(8,128)} fusion(f32[384,64,64]{2,1,0:T(8,128)} %bitcast.34, s32[1024]{0:T(1024)S(1)} %pad_clamp_fusion), kind=kCustom, calls=%fused_computation.1 | custom fusion | bytes 9438336 | tf_op jit(solution)/shard_map/gather | solution.py:23
  410.3 21.1 %convolution_bitcast_fusion = f32[288,64,64]{1,2,0:T(8,128)} fusion(f32[288,64,64]{2,1,0:T(8,128)} %gather_fusion.1, f32[288,64,64]{2,1,0:T(8,128)} %copy.9), kind=kOutput, calls=%fused_computation.2 | convolution fusion | flops 905969664 | bytes 14155776 | tf_op jit(solution)/shard_map/bji,bjk->bik/dot_general | solution.py:25
  431.4 11.6 %copy.15 = f32[288,64,64]{0,2,1:T(8,128)} copy(f32[288,64,64]{1,2,0:T(8,128)} %convolution_bitcast_fusion) | data formatting | bytes 9437184 | tf_op jit(solution)/shard_map/bji,bjk->bik/dot_general | solution.py:25
  443.0 5.9 %fusion.7 = f32[192,4096]{1,0:T(8,128)S(1)} fusion(f32[288,4096]{0,1:T(8,128)} %bitcast.30, s32[288]{0:T(512)S(1)} %get-tuple-element.8), kind=kOutput, calls=%fused_computation.18 | convolution fusion | flops 2717964288 | bytes 7865472 | tf_op jit(solution)/shard_map/dot_general | solution.py:29
  448.9 4.2 reshape.226
  453.2 0.0 reduce-scatter.5.cloned.1.call-update
  453.2 1.4 copy-done
  454.6 1.3 copy.16
  455.9 108.2 %reduce-scatter.5.cloned.1.call-done = f32[3072,64]{1,0:T(8,128)} async-done(((f32[12288,64]{1,0:T(8,128)}), f32[3072,64]{1,0:T(8,128)}) %reduce-scatter.5.cloned.1.call-update) | async-done | bytes 786448 | tf_op jit(solution)/shard_map/reduce_scatter | solution.py:63
  564.1 2.7 copy.17
  (20 shorter events, 0.2 us)
Async XLA Ops:
  7.2 123.7 %all-gather.3.cloned.1.call-start = ((), (), s32[]{:S(2)}) async-start(), calls=%async_computation.2 | async-start | bytes 7864320 | tf_op jit(solution)/shard_map/all_gather | solution.py:56
  12.7 272.8 %reduce-scatter.3.cloned.1.call-start = ((), (), s32[]{:S(2)}) async-start(), calls=%async_computation.3 | async-start | bytes 14155776 | tf_op jit(solution)/shard_map/reduce_scatter | solution.py:58
  19.0 12.3 %copy-start.2 = (s32[1,1,288]{2,1,0:T(1,128)S(1)}, s32[1,1,288]{2,1,0:T(1,128)}, u32[]{:S(2)}) copy-start(s32[1,1,288]{2,1,0:T(1,128)} %param.4) | copy-start | bytes 3460
  194.7 206.2 %all-gather.5.cloned.1.call-start = ((), (), s32[]{:S(2)}) async-start(), calls=%async_computation.4 | async-start | bytes 14155776 | tf_op jit(solution)/shard_map/all_gather | solution.py:61
  285.5 41.3 %copy-start.1 = (f32[3072,64]{1,0:T(8,128)S(1)}, f32[3072,64]{1,0:T(8,128)}, u32[]{:S(2)}) copy-start(f32[3072,64]{1,0:T(8,128)} %reduce-scatter.3.cloned.1.call-done) | copy-start | bytes 2359300
  328.1 236.0 %reduce-scatter.5.cloned.1.call-start = ((), (), s32[]{:S(2)}) async-start(), calls=%async_computation.5 | async-start | bytes 7864320 | tf_op jit(solution)/shard_map/reduce_scatter | solution.py:63
  453.2 1.4 copy-start
Sparse Core Ops, SparseCore 0:
  12.8 118.0 all-gather.2
  194.8 90.6 reduce-scatter.2
  328.2 72.6 all-gather.4
  453.3 110.7 reduce-scatter.4
where the time goes:
time: 574 us; the launch traced here: 573 us
  waiting for transfers between devices  371 us (65%)
  local copies, waits for them, and re-layouts  79.3 us (14%)
  matrix products  60.8 us (11%)
  blocking collectives  39.3 us (7%)
  between operations  13.9 us (2%)
  other arithmetic  8.73 us (2%)
    reduce_scatter x1, waiting for transfers between devices, local(): lax.psum_scatter(second_partial, 'col', scatter_dimension=0, tiled=True)  108 us
    all_gather x1, waiting for transfers between devices, local(): panel = lax.all_gather(own_panel, 'col', axis=0, tiled=True)  99.5 us
    reduce_scatter x1, waiting for transfers between devices, local(): lax.psum_scatter(partial_value, 'row', scatter_dimension=0, tiled=True)  90.7 us
    all_gather x1, waiting for transfers between devices, local(): normed_col_band = lax.all_gather(normed_own, 'row', axis=0, tiled=True)  72.7 us
    dot_general x2, matrix products, block_products(): jnp.einsum(pattern_text, tiles, picked, precision=lax.Precision.HIGHEST)  42.6 us
    psum x1, blocking collectives, local(): col_sums = lax.psum(jnp.sum(first_own * first_own, axis=0), ('row', 'col'))  39.3 us
    dot_general x2, local copies, waits for them, and re-layouts, block_products(): jnp.einsum(pattern_text, tiles, picked, precision=lax.Precision.HIGHEST)  23.2 us
    dot_general x2, matrix products, block_products(): jnp.dot(one_hot, products.reshape(tiles.shape[0], BLOCK * probe_count), p...  18.2 us
  transfers between devices with their start and end apart: 4, of which 4 were waited for; matrix products, arithmetic and copies ran while one was open for 3% of the time, Pallas kernels for 0%

commit v1 on v0

v1 whole, which is shorter than its diff:
```python
import functools

import jax
import jax.numpy as jnp
import numpy as np
from jax import lax
from jax.experimental import pallas as pl
from jax.experimental.pallas import tpu as pltpu
from jax.sharding import PartitionSpec as P

BLOCK = 64
PROBES = 64
HALF = BLOCK // 2
LANES = 128
MESH = pl.DeviceIdType.MESH
VMEM = pltpu.VMEM


def load_block(a_ref, group, lane):
    return a_ref[pl.ds(group * (8 * HALF) + lane, HALF, stride=8), :]


def signed_sums(col_blocks, slot_ref, a_ref, sign_ref, g_ref):
    g_ref[...] = jnp.zeros_like(g_ref)

    @pl.loop(0, a_ref.shape[0] // (8 * HALF))
    def _(group):
        terms = []
        for lane in range(8):
            slot = slot_ref[group * 8 + lane]
            i = lax.div(slot, col_blocks)
            j = slot - i * col_blocks
            terms.append((i, load_block(a_ref, group, lane) * sign_ref[pl.ds(j, 1), :]))
        for i, term in terms:
            g_ref[i] = g_ref[i] + term


def second_products(col_blocks, shard_blocks, slot_ref, a_ref, f_ref, inv_ref, p_ref):
    p_ref[...] = jnp.zeros_like(p_ref)
    inv = inv_ref[0:1, :]
    side = lax.broadcasted_iota(jnp.int32, (PROBES, LANES), 1) // BLOCK

    @pl.loop(0, a_ref.shape[0] // (8 * HALF))
    def _(group):
        terms = []
        for lane in range(8):
            slot = slot_ref[group * 8 + lane]
            i = lax.div(slot, col_blocks)
            j = slot - i * col_blocks
            shard = lax.div(j, shard_blocks)
            j = j - shard * shard_blocks
            pair = lax.div(j, 2)
            odd = j - 2 * pair
            a = pltpu.roll(load_block(a_ref, group, lane), odd * BLOCK, axis=1)
            n = f_ref[i] * inv
            ah = a.astype(jnp.bfloat16)
            al = (a - ah.astype(jnp.float32)).astype(jnp.bfloat16)
            nh = n.astype(jnp.bfloat16)
            nl = (n - nh.astype(jnp.float32)).astype(jnp.bfloat16)
            q = lax.dot_general(
                jnp.concatenate([nh, nl, nh], axis=0),
                jnp.concatenate([ah, ah, al], axis=0),
                (((0,), (0,)), ((), ())),
                preferred_element_type=jnp.float32,
            )
            r = q[:PROBES] + pltpu.roll(q[PROBES:], BLOCK, axis=1)
            terms.append((shard, pair, jnp.where(side == odd, r, 0.0)))
        for shard, pair, term in terms:
            where = pl.ds(pl.multiple_of(pair * LANES, LANES), LANES)
            p_ref[shard, :, where] = p_ref[shard, :, where] + term


def row_exchange(
    n_row, n_col, total_rows, g_ref, had_ref, fall_ref, normed_ref, inv_ref,
    recv, natural, cs_own, cs_mid, cs_row, cs_col,
    rs_send, rs_recv, ag_send, ag_recv, cr_send, cr_recv, cc_send, cc_recv,
):
    me = lax.axis_index("row")
    me_col = lax.axis_index("col")
    bits = n_row.bit_length() - 1
    rows = g_ref.shape[1]
    part = rows // 2
    orders = [list(range(bits)), [0] + list(range(bits - 1, 0, -1))]
    base = [sum(n_row >> (s + 1) for s in range(t)) for t in range(bits + 1)]

    barrier = pltpu.get_barrier_semaphore()
    for k in range(1, n_row):
        pl.semaphore_signal(barrier, inc=1, device_id=(me ^ k, me_col), device_id_type=MESH)
    for k in range(1, n_col):
        pl.semaphore_signal(barrier, inc=1, device_id=(me, me_col ^ k), device_id_type=MESH)
    pl.semaphore_wait(barrier, n_row + n_col - 2)

    def kept(h, s, m):
        left = orders[h][s + 1 :]
        mask = 0
        for pos, bit in enumerate(left):
            if not (m >> (len(left) - 1 - pos)) & 1:
                mask |= 1 << bit
        return mask

    def rs_copy(h, s, m):
        mask = kept(h, s, m) | (1 << orders[h][s])
        slot = base[s] + m
        if s == 0:
            source = g_ref.at[me ^ mask, pl.ds(h * part, part)]
        else:
            source = recv.at[h, base[s - 1] + m]
        return pltpu.make_async_remote_copy(
            src_ref=source,
            dst_ref=recv.at[h, slot],
            send_sem=rs_send.at[h, slot],
            recv_sem=rs_recv.at[h, slot],
            device_id=(me ^ (1 << orders[h][s]), me_col),
            device_id_type=MESH,
        )

    def take(h, s, m):
        rs_copy(h, s, m).wait_recv()
        if s == 0:
            mine = g_ref[me ^ kept(h, s, m), pl.ds(h * part, part)]
        else:
            mine = recv[h, base[s - 1] + (n_row >> (s + 1)) + m]
        recv[h, base[s] + m] = recv[h, base[s] + m] + mine

    for m in range(n_row // 2):
        for h in range(2):
            rs_copy(h, 0, m).start()
    for s in range(1, bits):
        count = n_row >> (s + 1)
        for m in range(count):
            for h in range(2):
                take(h, s - 1, m)
                rs_copy(h, s, m).start()
        for m in range(count):
            for h in range(2):
                take(h, s - 1, count + m)

    def held(h, u):
        masks = [0]
        for v in range(u):
            bit = 1 << orders[h][bits - 1 - v]
            masks = masks + [x | bit for x in masks]
        return masks

    def ag_copy(h, u, m):
        mask = held(h, u)[m]
        slot = (1 << u) - 1 + m
        where = fall_ref.at[me ^ mask, pl.ds(h * part, part)]
        return pltpu.make_async_remote_copy(
            src_ref=where,
            dst_ref=where,
            send_sem=ag_send.at[h, slot],
            recv_sem=ag_recv.at[h, slot],
            device_id=(me ^ (1 << orders[h][bits - 1 - u]), me_col),
            device_id_type=MESH,
        )

    cs_own[...] = jnp.zeros_like(cs_own)
    for h in range(2):
        take(h, bits - 1, 0)
        span = pl.ds(h * part, part)
        f = jnp.dot(
            recv[h, base[bits - 1]], had_ref[...],
            precision=lax.Precision.HIGHEST, preferred_element_type=jnp.float32,
        )
        fall_ref[me, span] = f
        for u in range(bits):
            ag_copy(h, u, 0).start()
        cs_own[...] += jnp.sum((f * f).reshape(part // 8, 8, LANES), axis=0)

    def cr_copy(k):
        return pltpu.make_async_remote_copy(
            src_ref=cs_own, dst_ref=cs_row.at[k], send_sem=cr_send.at[k], recv_sem=cr_recv.at[k],
            device_id=(me ^ k, me_col), device_id_type=MESH,
        )

    def cc_copy(k):
        return pltpu.make_async_remote_copy(
            src_ref=cs_mid, dst_ref=cs_col.at[k], send_sem=cc_send.at[k], recv_sem=cc_recv.at[k],
            device_id=(me, me_col ^ k), device_id_type=MESH,
        )

    for k in range(1, n_row):
        cr_copy(k).start()
    total = cs_own[...]
    for k in range(1, n_row):
        cr_copy(k).wait_recv()
        total = total + cs_row[k]
    cs_mid[...] = total
    for k in range(1, n_col):
        cc_copy(k).start()

    def arrived(h, u, m):
        ag_copy(h, u, m).wait_recv()
        got = held(h, u)[m] | (1 << orders[h][bits - 1 - u])
        for v in range(u + 1, bits):
            ag_copy(h, v, held(h, v).index(got)).start()

    for h in range(2):
        arrived(h, 0, 0)

    for k in range(1, n_col):
        cc_copy(k).wait_recv()
        total = total + cs_col[k]
    total = jnp.broadcast_to(jnp.sum(total, axis=0, keepdims=True), (8, LANES))
    total = total + pltpu.roll(total, BLOCK, axis=1)
    root = jnp.sqrt(total / total_rows + 1e-06)
    inv_ref[...] = 1.0 / root
    normed = fall_ref[me] / root[0:1, :]
    for side in range(2):
        natural[pl.ds(side, rows, stride=2), 0:BLOCK] = normed[:, side * BLOCK : (side + 1) * BLOCK]
    for t in range(0, 2 * rows, LANES):
        stop = min(t + LANES, 2 * rows)
        normed_ref[:, t:stop] = natural[t:stop, :].T[:PROBES]

    for u in range(1, bits):
        for m in range(1 << u):
            for h in range(2):
                arrived(h, u, m)

    for h in range(2):
        for s in range(bits):
            for m in range(n_row >> (s + 1)):
                rs_copy(h, s, m).wait_send()
        for u in range(bits):
            for m in range(1 << u):
                ag_copy(h, u, m).wait_send()
    for k in range(1, n_row):
        cr_copy(k).wait_send()
    for k in range(1, n_col):
        cc_copy(k).wait_send()


def col_reduce(n_col, p_ref, out_ref, recv, send_sem, recv_sem):
    me_row = lax.axis_index("row")
    me = lax.axis_index("col")
    width = out_ref.shape[1]

    barrier = pltpu.get_barrier_semaphore()

    @pl.when(me > 0)
    def _():
        pl.semaphore_signal(barrier, inc=1, device_id=(me_row, me - 1), device_id_type=MESH)

    @pl.when(me < n_col - 1)
    def _():
        pl.semaphore_signal(barrier, inc=1, device_id=(me_row, me + 1), device_id_type=MESH)

    pl.semaphore_wait(barrier, jnp.where(me == 0, 0, 1) + jnp.where(me == n_col - 1, 0, 1))

    def copy(way, d, own=False):
        return pltpu.make_async_remote_copy(
            src_ref=p_ref.at[d] if own else recv.at[way, d],
            dst_ref=recv.at[way, d],
            send_sem=send_sem.at[way, d],
            recv_sem=recv_sem.at[way, d],
            device_id=(me_row, me + 1 if way == 0 else me - 1),
            device_id_type=MESH,
        )

    def add(way, d):
        copy(way, d).wait_recv()
        recv[way, d] = recv[way, d] + p_ref[d]

    def step(way, d):
        first = 0 if way == 0 else n_col - 1

        @pl.when((me < d) if way == 0 else (me > d))
        def _():
            @pl.when(me != first)
            def _():
                add(way, d)
                copy(way, d).start()

            @pl.when(me == first)
            def _():
                copy(way, d, own=True).start()

    for t in range(n_col - 1):
        step(0, n_col - 1 - t)
        step(1, t)

    for d in range(n_col):

        @pl.when(me == d)
        def _():
            total = p_ref[d]
            if d > 0:
                copy(0, d).wait_recv()
                total = total + recv[0, d]
            if d < n_col - 1:
                copy(1, d).wait_recv()
                total = total + recv[1, d]
            out_ref[...] = total[:, :width]

    for d in range(n_col):

        @pl.when(me < d)
        def _():
            copy(0, d).wait_send()

        @pl.when(me > d)
        def _():
            copy(1, d).wait_send()


def vmem():
    return pl.BlockSpec(memory_space=VMEM)


def local(n_row, n_col, blocks, block_slot, sign_vec):
    local_rows = sign_vec.shape[0]
    total_rows = local_rows * n_row * n_col
    row_blocks = total_rows // n_col // BLOCK
    col_blocks = total_rows // n_row // BLOCK
    count = block_slot.shape[2]
    f32 = jnp.float32
    params = functools.partial(pltpu.CompilerParams, vmem_limit_bytes=48 * 1024 * 1024)

    tiles = blocks.reshape(count // 8, 8, HALF, LANES).transpose(0, 2, 1, 3).reshape(count * HALF, LANES)
    slots = block_slot.reshape(count)
    signs = lax.all_gather(sign_vec, "col", axis=0, tiled=True).astype(f32).reshape(col_blocks, BLOCK)
    signs = jnp.concatenate([signs, signs], axis=1)

    ids = np.arange(BLOCK)
    had = np.array([[1 - 2 * (bin(k & p).count("1") % 2) for p in ids] for k in ids], np.float32)
    had = jnp.asarray(np.kron(np.eye(2, dtype=np.float32), had))

    g = pl.pallas_call(
        functools.partial(signed_sums, col_blocks),
        out_shape=jax.ShapeDtypeStruct((row_blocks, HALF, LANES), f32),
        in_specs=[pl.BlockSpec(memory_space=pltpu.SMEM), vmem(), vmem()],
        out_specs=vmem(),
        compiler_params=params(),
        name="signed_sums",
    )(slots, tiles, signs)

    rows = local_rows // 2
    dma = pltpu.SemaphoreType.DMA
    fall, normed, inv = pl.pallas_call(
        functools.partial(row_exchange, n_row, n_col, float(total_rows)),
        out_shape=(
            jax.ShapeDtypeStruct((n_row, rows, LANES), f32),
            jax.ShapeDtypeStruct((PROBES, local_rows), f32),
            jax.ShapeDtypeStruct((8, LANES), f32),
        ),
        in_specs=[vmem(), vmem()],
        out_specs=(vmem(), vmem(), vmem()),
        scratch_shapes=[
            VMEM((2, n_row - 1, rows // 2, LANES), f32),
            VMEM((local_rows, LANES), f32),
            VMEM((8, LANES), f32),
            VMEM((8, LANES), f32),
            VMEM((n_row, 8, LANES), f32),
            VMEM((n_col, 8, LANES), f32),
            dma((2, n_row - 1)),
            dma((2, n_row - 1)),
            dma((2, n_row - 1)),
            dma((2, n_row - 1)),
            dma((n_row,)),
            dma((n_row,)),
            dma((n_col,)),
            dma((n_col,)),
        ],
        compiler_params=params(collective_id=0, has_side_effects=True),
        name="row_exchange",
    )(g.reshape(n_row, rows, LANES), had)

    width = -(-local_rows // LANES) * LANES
    second = pl.pallas_call(
        functools.partial(second_products, col_blocks, local_rows // BLOCK),
        out_shape=jax.ShapeDtypeStruct((n_col, PROBES, width), f32),
        in_specs=[pl.BlockSpec(memory_space=pltpu.SMEM), vmem(), vmem(), vmem()],
        out_specs=vmem(),
        compiler_params=params(),
        name="second_products",
    )(slots, tiles, fall.reshape(row_blocks, HALF, LANES), inv)

    power = pl.pallas_call(
        functools.partial(col_reduce, n_col),
        out_shape=jax.ShapeDtypeStruct((PROBES, local_rows), f32),
        in_specs=[vmem()],
        out_specs=vmem(),
        scratch_shapes=[
            VMEM((2, n_col, PROBES, width), f32),
            dma((2, n_col)),
            dma((2, n_col)),
        ],
        compiler_params=params(collective_id=1, has_side_effects=True),
        name="col_reduce",
    )(second)
    return normed.T, power.T


def solution(mesh):
    in_specs = (P("row", "col", None, None), P("row", "col", None), P(("col", "row")))
    out_specs = (P(("col", "row"), None), P(("col", "row"), None))
    body = functools.partial(local, mesh.shape["row"], mesh.shape["col"])
    return jax.shard_map(body, mesh=mesh, in_specs=in_specs, out_specs=out_specs, check_vma=False)
```

time: 574 us -> 190 us (0.33)
  waiting for transfers between devices: 371 us -> 0 us
  Pallas kernels: 0 us -> 170 us
  local copies, waits for them, and re-layouts: 79.3 us -> 4.18 us
  matrix products: 60.8 us -> 0 us
  blocking collectives: 39.3 us -> 15 us
  between operations: 13.9 us -> 0.68 us
  other arithmetic: 8.73 us -> 0.83 us
    reduce_scatter x2 -> x0, waiting for transfers between devices: 199 us -> none  [the longest x1 108 us: local(): lax.psum_scatter(second_partial, 'col', scatter_dimension=0, tiled=True)]
    all_gather x2 -> x0, waiting for transfers between devices: 172 us -> none  [the longest x1 99.5 us: local(): panel = lax.all_gather(own_panel, 'col', axis=0, tiled=True)]
    pallas_call x0 -> x4, Pallas kernels: none -> 170 us  [the longest x1 73 us: local(): pl.pallas_call(functools.partial(col_reduce, n_col), out_shape=jax.ShapeD...]
    dot_general x4 -> x0, matrix products: 60.8 us -> none  [the longest x2 42.6 us: block_products(): jnp.einsum(pattern_text, tiles, picked, precision=lax.Precision.HIGHEST)]
    psum x1 -> x0, blocking collectives: 39.3 us -> none  [local(): col_sums = lax.psum(jnp.sum(first_own * first_own, axis=0), ('row', 'col'))]
    reshape x3 -> x1, local copies, waits for them, and re-layouts: 27.4 us -> 0.08 us  [local(): lax.all_gather(sign_vec, 'col', axis=0, tiled=True).astype(f32)]
    dot_general x2 -> x0, local copies, waits for them, and re-layouts: 23.2 us -> none  [block_products(): jnp.einsum(pattern_text, tiles, picked, precision=lax.Precision.HIGHEST)]
    gather x2 -> x0, local copies, waits for them, and re-layouts: 17 us -> none  [block_products(): picked = field.reshape(-1, BLOCK, probe_count)[sources]]
  transfers between devices with their start and end apart: 4 -> 0, of which waited for: 4 -> 0; matrix products, arithmetic and copies ran while one was open for 3% -> 0% of each run, Pallas kernels for 0% -> 0%
where the time goes in v1:
time: 190 us
  Pallas kernels  170 us (89%)
  blocking collectives  15 us (8%)
  local copies, waits for them, and re-layouts  4.18 us (2%)
    pallas_call x1, Pallas kernels, local(): pl.pallas_call(functools.partial(col_reduce, n_col), out_shape=jax.ShapeD...  73 us
    pallas_call x1, Pallas kernels, local(): pl.pallas_call(functools.partial(row_exchange, n_row, n_col, float(total_...  70.8 us
    pallas_call x1, Pallas kernels, local(): pl.pallas_call(functools.partial(second_products, col_blocks, local_rows...  20.1 us
    all_gather x1, blocking collectives, local(): lax.all_gather(sign_vec, 'col', axis=0, tiled=True).astype(f32)  15 us
    pallas_call x1, Pallas kernels, local(): pl.pallas_call(functools.partial(signed_sums, col_blocks), out_shape=jax....  5.76 us
    unnamed x6, local copies, waits for them, and re-layouts  4.1 us

profile of v1, /device:TPU:0, one launch (start us, length us, event | category | flops | bytes accessed | tf_op | source)
XLA Modules:
  0.0 190.2 jit_solution(8074900875169944457)
XLA Ops:
  0.6 0.0 copy-start.1
  0.6 0.7 reduce.slot_ref
  1.4 15.0 %all_gather.3 = s32[12288]{0:T(1024)S(1)} all-gather(s32[3072]{0:T(1024)} %param.6), channel_id=1, replica_groups=mesh['row'=8,'col'=4] {'col'}, dimensions={0}, use_global_device_ids=true | all-gather | bytes 61440 | tf_op jit(solution)/shard_map/all_gather | solution.py:322
  16.3 0.1 reshape.25
  16.4 0.1 pad_maximum_fusion.sign_ref
  16.5 0.0 copy-start
  16.5 2.3 %copy-done = f32[1,1,288,4096]{3,2,1,0:T(8,128)S(1)} copy-done((f32[1,1,288,4096]{3,2,1,0:T(8,128)S(1)}, f32[1,1,288,4096]{3,2,1,0:T(8,128)}, u32[]{:S(2)}) %copy-start) | copy-done | bytes 4718616
  18.9 5.8 %signed_sums.1 = f32[384,32,128]{2,1,0:T(8,128)} custom-call(s32[288]{0:T(512)S(1)} %reduce.slot_ref, f32[9216,128]{1,0:T(8,128)S(1)} %bitcast.10, f32[192,128]{1,0:T(8,128)S(1)} %pad_maximum_fusion.sign_ref), custom_call_target="tpu_custom_call" | custom-call | tf_op jit(solution)/shard_map/signed_sums/pallas_call | solution.py:329
  24.6 0.0 copy-done.1
  24.6 70.8 %row_exchange.1 = (f32[8,1536,128]{2,1,0:T(8,128)}, f32[64,3072]{1,0:T(8,128)S(1)}, f32[8,128]{1,0:T(8,128)S(1)}) custom-call(f32[8,1536,128]{2,1,0:T(8,128)} %bitcast.13, f32[128,128]{1,0:T(8,128)S(1)} %copy-done.1), custom_call_target="tpu_custom_call" | custom-call | tf_op jit(solution)/shard_map/row_exchange/pallas_call | solution.py:340
  95.4 20.1 %second_products.1.p_ref = f32[4,64,3072]{2,1,0:T(8,128)S(1)} custom-call(s32[288]{0:T(512)S(1)} %reduce.slot_ref, f32[9216,128]{1,0:T(8,128)} %bitcast.9, f32[384,32,128]{2,1,0:T(8,128)} %bitcast.14, f32[8,128]{1,0:T(8,128)S(1)} %get-tuple-element.7.inv_ref), custom_call_target="tpu_custom_call" | custom-call | tf_op jit(solution)/shard_map/second_products/pallas_call | solution.py:370
  115.5 73.0 %col_reduce.1 = f32[64,3072]{1,0:T(8,128)S(1)} custom-call(f32[4,64,3072]{2,1,0:T(8,128)S(1)} %second_products.1.p_ref), custom_call_target="tpu_custom_call" | custom-call | tf_op jit(solution)/shard_map/col_reduce/pallas_call | solution.py:379
  188.5 0.9 copy.8
  189.4 0.9 copy.9
  (1 shorter events, 0.0 us)
Async XLA Ops:
  0.6 24.0 %copy-start.1 = (f32[128,128]{1,0:T(8,128)S(1)}, f32[128,128]{1,0:T(8,128)}, u32[]{:S(2)}) copy-start(f32[128,128]{1,0:T(8,128)} %constant.2.clone.had_ref) | copy-start | bytes 196612
  16.5 2.3 %copy-start = (f32[1,1,288,4096]{3,2,1,0:T(8,128)S(1)}, f32[1,1,288,4096]{3,2,1,0:T(8,128)}, u32[]{:S(2)}) copy-start(f32[1,1,288,4096]{3,2,1,0:T(8,128)} %param.4) | copy-start | bytes 14155780

commit v2 on v1

--- a/solution.py
+++ b/solution.py
@@ -12,6 +12,7 @@
 PROBES = 64
 HALF = BLOCK // 2
 LANES = 128
+PART = PROBES // 2
 MESH = pl.DeviceIdType.MESH
 VMEM = pltpu.VMEM
 
@@ -20,7 +21,28 @@
     return a_ref[pl.ds(group * (8 * HALF) + lane, HALF, stride=8), :]
 
 
-def signed_sums(col_blocks, slot_ref, a_ref, sign_ref, g_ref):
+def gather_signs(n_col, sign_ref, out_ref, send_sem, recv_sem):
+    me_row = lax.axis_index("row")
+    me = lax.axis_index("col")
+    barrier = pltpu.get_barrier_semaphore()
+    for k in range(1, n_col):
+        pl.semaphore_signal(barrier, inc=1, device_id=(me_row, me ^ k), device_id_type=MESH)
+    pl.semaphore_wait(barrier, n_col - 1)
+    copies = [
+        pltpu.make_async_remote_copy(
+            src_ref=sign_ref, dst_ref=out_ref.at[me], send_sem=send_sem.at[k], recv_sem=recv_sem.at[k],
+            device_id=(me_row, me ^ k), device_id_type=MESH,
+        )
+        for k in range(1, n_col)
+    ]
+    for copy in copies:
+        copy.start()
+    out_ref[me] = sign_ref[...]
+    for copy in copies:
+        copy.wait()
+
+
+def signed_sums(shard_blocks, col_blocks, slot_ref, a_ref, sign_ref, low_ref, high_ref, g_ref):
     g_ref[...] = jnp.zeros_like(g_ref)
 
     @pl.loop(0, a_ref.shape[0] // (8 * HALF))
@@ -30,15 +52,30 @@
             slot = slot_ref[group * 8 + lane]
             i = lax.div(slot, col_blocks)
             j = slot - i * col_blocks
-            terms.append((i, load_block(a_ref, group, lane) * sign_ref[pl.ds(j, 1), :]))
+            shard = lax.div(j, shard_blocks)
+            j = j - shard * shard_blocks
+            terms.append((i, load_block(a_ref, group, lane) * sign_ref[shard, pl.ds(j, 1), :]))
         for i, term in terms:
             g_ref[i] = g_ref[i] + term
+
+    lanes = lax.broadcasted_iota(jnp.int32, (HALF // 2, LANES), 1)
+    second = lanes // PART % 2 == 1
+
+    @pl.loop(0, g_ref.shape[0] // 8)
+    def _(group):
+        where = pl.ds(group * 8, 8)
+        g = g_ref[where]
+        first, last = g[:, : HALF // 2], g[:, HALF // 2 :]
+        mine = jnp.where(second, pltpu.roll(last, PART, axis=2), first)
+        other = jnp.where(second, last, pltpu.roll(first, LANES - PART, axis=2))
+        low_ref[where] = mine + other
+        high_ref[where] = mine - other
 
 
 def second_products(col_blocks, shard_blocks, slot_ref, a_ref, f_ref, inv_ref, p_ref):
     p_ref[...] = jnp.zeros_like(p_ref)
     inv = inv_ref[0:1, :]
-    side = lax.broadcasted_iota(jnp.int32, (PROBES, LANES), 1) // BLOCK
+    side = lax.broadcasted_iota(jnp.int32, (PART, LANES), 1) // BLOCK
 
     @pl.loop(0, a_ref.shape[0] // (8 * HALF))
     def _(group):
@@ -51,7 +88,8 @@
             j = j - shard * shard_blocks
             pair = lax.div(j, 2)
             odd = j - 2 * pair
-            a = pltpu.roll(load_block(a_ref, group, lane), odd * BLOCK, axis=1)
+            a = load_block(a_ref, group, lane)
+            a = jnp.concatenate([a[: HALF // 2], a[HALF // 2 :]], axis=1)
             n = f_ref[i] * inv
             ah = a.astype(jnp.bfloat16)
             al = (a - ah.astype(jnp.float32)).astype(jnp.bfloat16)
@@ -63,18 +101,89 @@
                 (((0,), (0,)), ((), ())),
                 preferred_element_type=jnp.float32,
             )
-            r = q[:PROBES] + pltpu.roll(q[PROBES:], BLOCK, axis=1)
+            q0 = q[:PART, :LANES] + q[PART : 2 * PART, LANES:]
+            q1 = q[2 * PART : 3 * PART, :LANES] + q[3 * PART :, LANES:]
+            r = jnp.where(odd == 1, q1, q0) + pltpu.roll(jnp.where(odd == 1, q0, q1), BLOCK, axis=1)
             terms.append((shard, pair, jnp.where(side == odd, r, 0.0)))
         for shard, pair, term in terms:
             where = pl.ds(pl.multiple_of(pair * LANES, LANES), LANES)
             p_ref[shard, :, where] = p_ref[shard, :, where] + term
 
 
-def row_exchange(
-    n_row, n_col, total_rows, g_ref, had_ref, fall_ref, normed_ref, inv_ref,
-    recv, natural, cs_own, cs_mid, cs_row, cs_col,
-    rs_send, rs_recv, ag_send, ag_recv, cr_send, cr_recv, cc_send, cc_recv,
-):
+def line_steps(n_col, p_ref, out_ref, recv, send_sem, recv_sem):
+    me_row = lax.axis_index("row")
+    me = lax.axis_index("col")
+    width = out_ref.shape[1]
+
+    def copy(way, d, own=False):
+        return pltpu.make_async_remote_copy(
+            src_ref=p_ref.at[d] if own else recv.at[way, d],
+            dst_ref=recv.at[way, d],
+            send_sem=send_sem.at[way, d],
+            recv_sem=recv_sem.at[way, d],
+            device_id=(me_row, me + 1 if way == 0 else me - 1),
+            device_id_type=MESH,
+        )
+
+    def begin():
+        @pl.when(me == 0)
+        def _():
+            for d in range(n_col - 1, 0, -1):
+                copy(0, d, own=True).start()
+
+        @pl.when(me == n_col - 1)
+        def _():
+            for d in range(n_col - 1):
+                copy(1, d, own=True).start()
+
+    def relay(t):
+        for way, d in ((0, n_col - 1 - t), (1, t)):
+
+            @pl.when((me > 0) & (me < d) if way == 0 else (me < n_col - 1) & (me > d))
+            def _():
+                copy(way, d).wait_recv()
+                recv[way, d] = recv[way, d] + p_ref[d]
+                copy(way, d).start()
+
+    def finish():
+        for d in range(n_col):
+
+            @pl.when(me == d)
+            def _():
+                total = p_ref[d]
+                if d > 0:
+                    copy(0, d).wait_recv()
+                    total = total + recv[0, d]
+                if d < n_col - 1:
+                    copy(1, d).wait_recv()
+                    total = total + recv[1, d]
+                out_ref[...] = total[:, :width]
+
+        for d in range(n_col):
+
+            @pl.when(me < d)
+            def _():
+                copy(0, d).wait_send()
+
+            @pl.when(me > d)
+            def _():
+                copy(1, d).wait_send()
+
+    return begin, relay, finish
+
+
+def row_exchange(n_row, n_col, total_rows, both, *refs):
+    if both:
+        g_ref, had_ref, p_ref, fall_ref, normed_ref, inv_ref, power_ref = refs[:7]
+        refs = refs[7:]
+        begin, relay, finish = line_steps(n_col, p_ref, power_ref, *refs[-3:])
+        refs = refs[:-3]
+    else:
+        g_ref, had_ref, fall_ref, normed_ref, inv_ref = refs[:5]
+        refs = refs[5:]
+        begin, relay, finish = lambda: None, lambda t: None, lambda: None
+    recv, natural, cs_own, cs_mid, cs_row, cs_col = refs[:6]
+    rs_send, rs_recv, ag_send, ag_recv, cr_send, cr_recv, cc_send, cc_recv = refs[6:]
     me = lax.axis_index("row")
     me_col = lax.axis_index("col")
     bits = n_row.bit_length() - 1
@@ -122,6 +231,7 @@
             mine = recv[h, base[s - 1] + (n_row >> (s + 1)) + m]
         recv[h, base[s] + m] = recv[h, base[s] + m] + mine
 
+    begin()
     for m in range(n_row // 2):
         for h in range(2):
             rs_copy(h, 0, m).start()
@@ -155,6 +265,7 @@
             device_id_type=MESH,
         )
 
+    relay(0)
     cs_own[...] = jnp.zeros_like(cs_own)
     for h in range(2):
         take(h, bits - 1, 0)
@@ -204,15 +315,23 @@
         total = total + cs_col[k]
     total = jnp.broadcast_to(jnp.sum(total, axis=0, keepdims=True), (8, LANES))
     total = total + pltpu.roll(total, BLOCK, axis=1)
+    total = total + pltpu.roll(total, PART, axis=1)
     root = jnp.sqrt(total / total_rows + 1e-06)
     inv_ref[...] = 1.0 / root
     normed = fall_ref[me] / root[0:1, :]
-    for side in range(2):
-        natural[pl.ds(side, rows, stride=2), 0:BLOCK] = normed[:, side * BLOCK : (side + 1) * BLOCK]
-    for t in range(0, 2 * rows, LANES):
-        stop = min(t + LANES, 2 * rows)
-        normed_ref[:, t:stop] = natural[t:stop, :].T[:PROBES]
-
+    blocks = rows // (HALF // 2)
+    for h in range(2):
+        for u in range(2):
+            lane = (2 * h + u) * PART
+            piece = normed[:, lane : lane + PART].reshape(blocks, HALF // 2, PART)
+            for i in range(blocks):
+                natural[pl.ds(i * BLOCK + u * HALF + h, HALF // 2, stride=2), 0:PART] = piece[i]
+    for t in range(0, blocks * BLOCK, LANES):
+        stop = min(t + LANES, blocks * BLOCK)
+        normed_ref[:, t:stop] = natural[t:stop, :].T[:PART]
+
+    for t in range(1, n_col - 1):
+        relay(t)
     for u in range(1, bits):
         for m in range(1 << u):
             for h in range(2):
@@ -229,13 +348,12 @@
         cr_copy(k).wait_send()
     for k in range(1, n_col):
         cc_copy(k).wait_send()
+    finish()
 
 
 def col_reduce(n_col, p_ref, out_ref, recv, send_sem, recv_sem):
     me_row = lax.axis_index("row")
     me = lax.axis_index("col")
-    width = out_ref.shape[1]
-
     barrier = pltpu.get_barrier_semaphore()
 
     @pl.when(me > 0)
@@ -248,60 +366,11 @@
 
     pl.semaphore_wait(barrier, jnp.where(me == 0, 0, 1) + jnp.where(me == n_col - 1, 0, 1))
 
-    def copy(way, d, own=False):
-        return pltpu.make_async_remote_copy(
-            src_ref=p_ref.at[d] if own else recv.at[way, d],
-            dst_ref=recv.at[way, d],
-            send_sem=send_sem.at[way, d],
-            recv_sem=recv_sem.at[way, d],
-            device_id=(me_row, me + 1 if way == 0 else me - 1),
-            device_id_type=MESH,
-        )
-
-    def add(way, d):
-        copy(way, d).wait_recv()
-        recv[way, d] = recv[way, d] + p_ref[d]
-
-    def step(way, d):
-        first = 0 if way == 0 else n_col - 1
-
-        @pl.when((me < d) if way == 0 else (me > d))
-        def _():
-            @pl.when(me != first)
-            def _():
-                add(way, d)
-                copy(way, d).start()
-
-            @pl.when(me == first)
-            def _():
-                copy(way, d, own=True).start()
-
+    begin, relay, finish = line_steps(n_col, p_ref, out_ref, recv, send_sem, recv_sem)
+    begin()
     for t in range(n_col - 1):
-        step(0, n_col - 1 - t)
-        step(1, t)
-
-    for d in range(n_col):
-
-        @pl.when(me == d)
-        def _():
-            total = p_ref[d]
-            if d > 0:
-                copy(0, d).wait_recv()
-                total = total + recv[0, d]
-            if d < n_col - 1:
-                copy(1, d).wait_recv()
-                total = total + recv[1, d]
-            out_ref[...] = total[:, :width]
-
-    for d in range(n_col):
-
-        @pl.when(me < d)
-        def _():
-            copy(0, d).wait_send()
-
-        @pl.when(me > d)
-        def _():
-            copy(1, d).wait_send()
+        relay(t)
+    finish()
 
 
 def vmem():
@@ -319,77 +388,94 @@
 
     tiles = blocks.reshape(count // 8, 8, HALF, LANES).transpose(0, 2, 1, 3).reshape(count * HALF, LANES)
     slots = block_slot.reshape(count)
-    signs = lax.all_gather(sign_vec, "col", axis=0, tiled=True).astype(f32).reshape(col_blocks, BLOCK)
-    signs = jnp.concatenate([signs, signs], axis=1)
-
-    ids = np.arange(BLOCK)
+    dma = pltpu.SemaphoreType.DMA
+
+    def comm(index, **kw):
+        return params(collective_id=index, has_side_effects=True, **kw)
+
+    shard_blocks = local_rows // BLOCK
+    signs = sign_vec.astype(f32).reshape(shard_blocks, BLOCK)
+    signs = pl.pallas_call(
+        functools.partial(gather_signs, n_col),
+        out_shape=jax.ShapeDtypeStruct((n_col, shard_blocks, LANES), f32),
+        in_specs=[vmem()],
+        out_specs=vmem(),
+        scratch_shapes=[dma((n_col,)), dma((n_col,))],
+        compiler_params=comm(0),
+        name="gather_signs",
+    )(jnp.concatenate([signs, signs], axis=1))
+
+    ids = np.arange(PART)
     had = np.array([[1 - 2 * (bin(k & p).count("1") % 2) for p in ids] for k in ids], np.float32)
-    had = jnp.asarray(np.kron(np.eye(2, dtype=np.float32), had))
-
-    g = pl.pallas_call(
-        functools.partial(signed_sums, col_blocks),
-        out_shape=jax.ShapeDtypeStruct((row_blocks, HALF, LANES), f32),
+    had = jnp.asarray(np.kron(np.eye(4, dtype=np.float32), had))
+
+    halves = pl.pallas_call(
+        functools.partial(signed_sums, shard_blocks, col_blocks),
+        out_shape=(jax.ShapeDtypeStruct((row_blocks, HALF // 2, LANES), f32),) * 2,
         in_specs=[pl.BlockSpec(memory_space=pltpu.SMEM), vmem(), vmem()],
-        out_specs=vmem(),
+        out_specs=(vmem(), vmem()),
+        scratch_shapes=[VMEM((row_blocks, HALF, LANES), f32)],
         compiler_params=params(),
         name="signed_sums",
     )(slots, tiles, signs)
 
-    rows = local_rows // 2
-    dma = pltpu.SemaphoreType.DMA
-    fall, normed, inv = pl.pallas_call(
-        functools.partial(row_exchange, n_row, n_col, float(total_rows)),
-        out_shape=(
-            jax.ShapeDtypeStruct((n_row, rows, LANES), f32),
-            jax.ShapeDtypeStruct((PROBES, local_rows), f32),
-            jax.ShapeDtypeStruct((8, LANES), f32),
-        ),
-        in_specs=[vmem(), vmem()],
-        out_specs=(vmem(), vmem(), vmem()),
-        scratch_shapes=[
-            VMEM((2, n_row - 1, rows // 2, LANES), f32),
-            VMEM((local_rows, LANES), f32),
-            VMEM((8, LANES), f32),
-            VMEM((8, LANES), f32),
-            VMEM((n_row, 8, LANES), f32),
-            VMEM((n_col, 8, LANES), f32),
-            dma((2, n_row - 1)),
-            dma((2, n_row - 1)),
-            dma((2, n_row - 1)),
-            dma((2, n_row - 1)),
-            dma((n_row,)),
-            dma((n_row,)),
-            dma((n_col,)),
-            dma((n_col,)),
-        ],
-        compiler_params=params(collective_id=0, has_side_effects=True),
-        name="row_exchange",
-    )(g.reshape(n_row, rows, LANES), had)
-
+    rows = local_rows // 4
     width = -(-local_rows // LANES) * LANES
-    second = pl.pallas_call(
-        functools.partial(second_products, col_blocks, local_rows // BLOCK),
-        out_shape=jax.ShapeDtypeStruct((n_col, PROBES, width), f32),
-        in_specs=[pl.BlockSpec(memory_space=pltpu.SMEM), vmem(), vmem(), vmem()],
-        out_specs=vmem(),
-        compiler_params=params(),
-        name="second_products",
-    )(slots, tiles, fall.reshape(row_blocks, HALF, LANES), inv)
-
-    power = pl.pallas_call(
-        functools.partial(col_reduce, n_col),
-        out_shape=jax.ShapeDtypeStruct((PROBES, local_rows), f32),
-        in_specs=[vmem()],
-        out_specs=vmem(),
-        scratch_shapes=[
-            VMEM((2, n_col, PROBES, width), f32),
-            dma((2, n_col)),
-            dma((2, n_col)),
-        ],
-        compiler_params=params(collective_id=1, has_side_effects=True),
-        name="col_reduce",
-    )(second)
-    return normed.T, power.T
+    row_scratch = [
+        VMEM((2, n_row - 1, rows // 2, LANES), f32),
+        VMEM((local_rows, LANES), f32),
+        VMEM((8, LANES), f32),
+        VMEM((8, LANES), f32),
+        VMEM((n_row, 8, LANES), f32),
+        VMEM((n_col, 8, LANES), f32),
+        *[dma((2, n_row - 1))] * 4,
+        *[dma((n_row,))] * 2,
+        *[dma((n_col,))] * 2,
+    ]
+    line_scratch = [VMEM((2, n_col, PART, width), f32), dma((2, n_col)), dma((2, n_col))]
+    own_part = jax.ShapeDtypeStruct((PART, local_rows), f32)
+
+    normed, power = [], []
+    second = None
+    for half in range(2):
+        both = half > 0
+        outs = pl.pallas_call(
+            functools.partial(row_exchange, n_row, n_col, float(total_rows), both),
+            out_shape=(
+                jax.ShapeDtypeStruct((n_row, rows, LANES), f32),
+                own_part,
+                jax.ShapeDtypeStruct((8, LANES), f32),
+            )
+            + (own_part,) * both,
+            in_specs=[vmem()] * (2 + both),
+            out_specs=(vmem(),) * (3 + both),
+            scratch_shapes=row_scratch + line_scratch * both,
+            compiler_params=comm(1 + half),
+            name="row_exchange",
+        )(halves[half].reshape(n_row, rows, LANES), had, *([second] * both))
+        normed.append(outs[1])
+        power.extend(outs[3:])
+        second = pl.pallas_call(
+            functools.partial(second_products, col_blocks, shard_blocks),
+            out_shape=jax.ShapeDtypeStruct((n_col, PART, width), f32),
+            in_specs=[pl.BlockSpec(memory_space=pltpu.SMEM), vmem(), vmem(), vmem()],
+            out_specs=vmem(),
+            compiler_params=params(),
+            name="second_products",
+        )(slots, tiles, outs[0].reshape(row_blocks, HALF // 2, LANES), outs[2])
+
+    power.append(
+        pl.pallas_call(
+            functools.partial(col_reduce, n_col),
+            out_shape=own_part,
+            in_specs=[vmem()],
+            out_specs=vmem(),
+            scratch_shapes=line_scratch,
+            compiler_params=comm(3),
+            name="col_reduce",
+        )(second)
+    )
+    return jnp.concatenate(normed, axis=0).T, jnp.concatenate(power, axis=0).T
 
 
 def solution(mesh):

time: 190 us -> 196 us (1.032)
  Pallas kernels: 170 us -> 190 us
  blocking collectives: 15 us -> 0 us
  local copies, waits for them, and re-layouts: 4.18 us -> 1.76 us
  other arithmetic: 0.83 us -> 2.79 us
    pallas_call x1 -> x2, Pallas kernels: 70.8 us -> 91.9 us  [local(): pl.pallas_call(functools.partial(row_exchange, n_row, n_col, float(total_...]
    all_gather x1 -> x0, blocking collectives: 15 us -> none  [local(): lax.all_gather(sign_vec, 'col', axis=0, tiled=True).astype(f32)]
    unnamed x6 -> x4, local copies, waits for them, and re-layouts: 4.1 us -> 1.69 us
    pallas_call x3 -> x5, Pallas kernels: 98.8 us -> 98.2 us  [the longest x1 42.9 us: local(): pl.pallas_call(functools.partial(col_reduce, n_col), out_shape=own_part,...]
where the time goes in v2:
time: 196 us; the launch traced here: 195 us
  Pallas kernels  190 us (97%)
  other arithmetic  2.79 us (1%)
    pallas_call x2, Pallas kernels, local(): pl.pallas_call(functools.partial(row_exchange, n_row, n_col, float(total_...  91.9 us
    pallas_call x1, Pallas kernels, local(): pl.pallas_call(functools.partial(col_reduce, n_col), out_shape=own_part,...  42.9 us
    pallas_call x2, Pallas kernels, local(): pl.pallas_call(functools.partial(second_products, col_blocks, shard_block...  35.2 us
    pallas_call x1, Pallas kernels, local(): pl.pallas_call(functools.partial(signed_sums, shard_blocks, col_blocks),...  12.1 us
    pallas_call x1, Pallas kernels, local(): pl.pallas_call(functools.partial(gather_signs, n_col), out_shape=jax.Shap...  8.02 us

profile of v2, /device:TPU:0, one launch (start us, length us, event | category | flops | bytes accessed | tf_op | source)
XLA Modules:
  0.0 195.3 jit_solution(11444550449571221954)
XLA Ops:
  0.6 0.0 copy-start.1
  0.6 0.7 reduce.slot_ref
  1.4 0.7 convert_element_type.3
  2.1 0.1 reshape.31
  2.2 0.1 pad_maximum_fusion.sign_ref
  2.2 8.0 %gather_signs.1.sign_ref = f32[4,48,128]{2,1,0:T(8,128)S(1)} custom-call(f32[48,128]{1,0:T(8,128)S(1)} %pad_maximum_fusion.sign_ref), custom_call_target="tpu_custom_call" | custom-call | tf_op jit(solution)/shard_map/gather_signs/pallas_call | solution.py:398
  10.3 12.1 %signed_sums.1 = (f32[384,16,128]{2,1,0:T(8,128)S(1)}, f32[384,16,128]{2,1,0:T(8,128)}) custom-call(s32[288]{0:T(512)S(1)} %reduce.slot_ref, f32[9216,128]{1,0:T(8,128)} %bitcast.16, f32[4,48,128]{2,1,0:T(8,128)S(1)} %gather_signs.1.sign_ref), custom_call_target="tpu_custom_call" | custom-call | tf_op jit(solution)/shard_map/signed_sums/pallas_call | solution.py:412
  22.3 0.0 copy-start
  22.3 1.7 copy-done
  24.0 0.0 copy-done.1
  24.0 40.5 %row_exchange.2 = (f32[8,768,128]{2,1,0:T(8,128)S(1)}, f32[32,3072]{1,0:T(8,128)S(1)}, f32[8,128]{1,0:T(8,128)S(1)}) custom-call(f32[8,768,128]{2,1,0:T(8,128)} %bitcast.13, f32[128,128]{1,0:T(8,128)S(1)} %copy-done.1), custom_call_target="tpu_custom_call" | custom-call | tf_op jit(solution)/shard_map/row_exchange/pallas_call | solution.py:442
  64.5 17.6 %second_products.2.refs_2_ = f32[4,32,3072]{2,1,0:T(8,128)S(1)} custom-call(s32[288]{0:T(512)S(1)} %reduce.slot_ref, f32[9216,128]{1,0:T(8,128)} %bitcast.17, f32[384,16,128]{2,1,0:T(8,128)S(1)} %bitcast.15, f32[8,128]{1,0:T(8,128)S(1)} %get-tuple-element.15.inv_ref), custom_call_target="tpu_custom_call" | custom-call | tf_op jit(solution)/shard_map/second_products/pallas_call | solution.py:458
  82.2 51.4 %row_exchange.3 = (f32[8,768,128]{2,1,0:T(8,128)S(1)}, f32[32,3072]{1,0:T(8,128)S(1)}, f32[8,128]{1,0:T(8,128)S(1)}, f32[32,3072]{1,0:T(8,128)S(1)}) custom-call(f32[8,768,128]{2,1,0:T(8,128)} %bitcast.19, f32[128,128]{1,0:T(8,128)S(1)} %copy-done.1, f32[4,32,3072]{2,1,0:T(8,128)S(1)} %second_products.2.refs_2_), custom_call_target="tpu_custom_call" | custom-call | tf_op jit(solution)/shard_map/row_exchange/pallas_call | solution.py:442
  133.6 17.6 %second_products.3.p_ref = f32[4,32,3072]{2,1,0:T(8,128)S(1)} custom-call(s32[288]{0:T(512)S(1)} %reduce.slot_ref, f32[9216,128]{1,0:T(8,128)} %bitcast.18, f32[384,16,128]{2,1,0:T(8,128)S(1)} %bitcast.14, f32[8,128]{1,0:T(8,128)S(1)} %get-tuple-element.19.inv_ref), custom_call_target="tpu_custom_call" | custom-call | tf_op jit(solution)/shard_map/second_products/pallas_call | solution.py:458
  151.2 42.9 %col_reduce.1 = f32[32,3072]{1,0:T(8,128)S(1)} custom-call(f32[4,32,3072]{2,1,0:T(8,128)S(1)} %second_products.3.p_ref), custom_call_target="tpu_custom_call" | custom-call | tf_op jit(solution)/shard_map/col_reduce/pallas_call | solution.py:468
  194.0 1.3 maximum_bitcast_fusion
Async XLA Ops:
  0.6 23.4 %copy-start.1 = (f32[128,128]{1,0:T(8,128)S(1)}, f32[128,128]{1,0:T(8,128)}, u32[]{:S(2)}) copy-start(f32[128,128]{1,0:T(8,128)} %constant.2.clone.refs_1_) | copy-start | bytes 196612
  22.3 1.7 copy-start

commit v3 on v1

--- a/solution.py
+++ b/solution.py
@@ -20,7 +20,28 @@
     return a_ref[pl.ds(group * (8 * HALF) + lane, HALF, stride=8), :]
 
 
-def signed_sums(col_blocks, slot_ref, a_ref, sign_ref, g_ref):
+def gather_signs(n_col, sign_ref, out_ref, send_sem, recv_sem):
+    me_row = lax.axis_index("row")
+    me = lax.axis_index("col")
+    barrier = pltpu.get_barrier_semaphore()
+    for k in range(1, n_col):
+        pl.semaphore_signal(barrier, inc=1, device_id=(me_row, me ^ k), device_id_type=MESH)
+    pl.semaphore_wait(barrier, n_col - 1)
+    copies = [
+        pltpu.make_async_remote_copy(
+            src_ref=sign_ref, dst_ref=out_ref.at[me], send_sem=send_sem.at[k], recv_sem=recv_sem.at[k],
+            device_id=(me_row, me ^ k), device_id_type=MESH,
+        )
+        for k in range(1, n_col)
+    ]
+    for copy in copies:
+        copy.start()
+    out_ref[me] = sign_ref[...]
+    for copy in copies:
+        copy.wait()
+
+
+def signed_sums(shard_blocks, col_blocks, slot_ref, a_ref, sign_ref, g_ref):
     g_ref[...] = jnp.zeros_like(g_ref)
 
     @pl.loop(0, a_ref.shape[0] // (8 * HALF))
@@ -30,7 +51,9 @@
             slot = slot_ref[group * 8 + lane]
             i = lax.div(slot, col_blocks)
             j = slot - i * col_blocks
-            terms.append((i, load_block(a_ref, group, lane) * sign_ref[pl.ds(j, 1), :]))
+            shard = lax.div(j, shard_blocks)
+            j = j - shard * shard_blocks
+            terms.append((i, load_block(a_ref, group, lane) * sign_ref[shard, pl.ds(j, 1), :]))
         for i, term in terms:
             g_ref[i] = g_ref[i] + term
 
@@ -319,15 +342,29 @@
 
     tiles = blocks.reshape(count // 8, 8, HALF, LANES).transpose(0, 2, 1, 3).reshape(count * HALF, LANES)
     slots = block_slot.reshape(count)
-    signs = lax.all_gather(sign_vec, "col", axis=0, tiled=True).astype(f32).reshape(col_blocks, BLOCK)
-    signs = jnp.concatenate([signs, signs], axis=1)
+    dma = pltpu.SemaphoreType.DMA
+
+    def comm(index, **kw):
+        return params(collective_id=index, has_side_effects=True, **kw)
+
+    shard_blocks = local_rows // BLOCK
+    signs = sign_vec.astype(f32).reshape(shard_blocks, BLOCK)
+    signs = pl.pallas_call(
+        functools.partial(gather_signs, n_col),
+        out_shape=jax.ShapeDtypeStruct((n_col, shard_blocks, LANES), f32),
+        in_specs=[vmem()],
+        out_specs=vmem(),
+        scratch_shapes=[dma((n_col,)), dma((n_col,))],
+        compiler_params=comm(0),
+        name="gather_signs",
+    )(jnp.concatenate([signs, signs], axis=1))
 
     ids = np.arange(BLOCK)
     had = np.array([[1 - 2 * (bin(k & p).count("1") % 2) for p in ids] for k in ids], np.float32)
     had = jnp.asarray(np.kron(np.eye(2, dtype=np.float32), had))
 
     g = pl.pallas_call(
-        functools.partial(signed_sums, col_blocks),
+        functools.partial(signed_sums, shard_blocks, col_blocks),
         out_shape=jax.ShapeDtypeStruct((row_blocks, HALF, LANES), f32),
         in_specs=[pl.BlockSpec(memory_space=pltpu.SMEM), vmem(), vmem()],
         out_specs=vmem(),
@@ -336,7 +373,6 @@
     )(slots, tiles, signs)
 
     rows = local_rows // 2
-    dma = pltpu.SemaphoreType.DMA
     fall, normed, inv = pl.pallas_call(
         functools.partial(row_exchange, n_row, n_col, float(total_rows)),
         out_shape=(
@@ -362,7 +398,7 @@
             dma((n_col,)),
             dma((n_col,)),
         ],
-        compiler_params=params(collective_id=0, has_side_effects=True),
+        compiler_params=comm(1),
         name="row_exchange",
     )(g.reshape(n_row, rows, LANES), had)
 
@@ -386,7 +422,7 @@
             dma((2, n_col)),
             dma((2, n_col)),
         ],
-        compiler_params=params(collective_id=1, has_side_effects=True),
+        compiler_params=comm(2),
         name="col_reduce",
     )(second)
     return normed.T, power.T

time: 190 us -> 184 us (0.968)
  blocking collectives: 15 us -> 0 us
  Pallas kernels: 170 us -> 178 us
    all_gather x1 -> x0, blocking collectives: 15 us -> none  [local(): lax.all_gather(sign_vec, 'col', axis=0, tiled=True).astype(f32)]
    pallas_call x1 -> x2, Pallas kernels: 5.76 us -> 14.1 us  [the longest x1 8.02 us: local(): pl.pallas_call(functools.partial(gather_signs, n_col), out_shape=jax.Shap...]
where the time goes in v3:
time: 184 us
  Pallas kernels  178 us (97%)
  local copies, waits for them, and re-layouts  4.17 us (2%)
    pallas_call x1, Pallas kernels, local(): pl.pallas_call(functools.partial(col_reduce, n_col), out_shape=jax.ShapeD...  72.8 us
    pallas_call x1, Pallas kernels, local(): pl.pallas_call(functools.partial(row_exchange, n_row, n_col, float(total_...  70.8 us
    pallas_call x1, Pallas kernels, local(): pl.pallas_call(functools.partial(second_products, col_blocks, local_rows...  20.1 us
    pallas_call x1, Pallas kernels, local(): pl.pallas_call(functools.partial(gather_signs, n_col), out_shape=jax.Shap...  8.02 us
    pallas_call x1, Pallas kernels, local(): pl.pallas_call(functools.partial(signed_sums, shard_blocks, col_blocks),...  6.12 us
    unnamed x6, local copies, waits for them, and re-layouts  4.1 us

profile of v3, /device:TPU:0, one launch (start us, length us, event | category | flops | bytes accessed | tf_op | source)
XLA Modules:
  0.0 184.1 jit_solution(16924338403400554926)
XLA Ops:
  0.6 0.0 copy-start.1
  0.6 0.7 reduce.slot_ref
  1.4 0.7 convert_element_type.3
  2.1 0.1 reshape.25
  2.2 0.1 pad_maximum_fusion.sign_ref
  2.2 8.0 %gather_signs.1.sign_ref = f32[4,48,128]{2,1,0:T(8,128)S(1)} custom-call(f32[48,128]{1,0:T(8,128)S(1)} %pad_maximum_fusion.sign_ref), custom_call_target="tpu_custom_call" | custom-call | tf_op jit(solution)/shard_map/gather_signs/pallas_call | solution.py:352
  10.3 0.0 copy-start
  10.3 2.3 %copy-done = f32[1,1,288,4096]{3,2,1,0:T(8,128)S(1)} copy-done((f32[1,1,288,4096]{3,2,1,0:T(8,128)S(1)}, f32[1,1,288,4096]{3,2,1,0:T(8,128)}, u32[]{:S(2)}) %copy-start) | copy-done | bytes 4718616
  12.6 6.1 %signed_sums.1 = f32[384,32,128]{2,1,0:T(8,128)} custom-call(s32[288]{0:T(512)S(1)} %reduce.slot_ref, f32[9216,128]{1,0:T(8,128)S(1)} %bitcast.10, f32[4,48,128]{2,1,0:T(8,128)S(1)} %gather_signs.1.sign_ref), custom_call_target="tpu_custom_call" | custom-call | tf_op jit(solution)/shard_map/signed_sums/pallas_call | solution.py:366
  18.7 0.0 copy-done.1
  18.7 70.8 %row_exchange.1 = (f32[8,1536,128]{2,1,0:T(8,128)}, f32[64,3072]{1,0:T(8,128)S(1)}, f32[8,128]{1,0:T(8,128)S(1)}) custom-call(f32[8,1536,128]{2,1,0:T(8,128)} %bitcast.13, f32[128,128]{1,0:T(8,128)S(1)} %copy-done.1), custom_call_target="tpu_custom_call" | custom-call | tf_op jit(solution)/shard_map/row_exchange/pallas_call | solution.py:376
  89.5 20.1 %second_products.1.p_ref = f32[4,64,3072]{2,1,0:T(8,128)S(1)} custom-call(s32[288]{0:T(512)S(1)} %reduce.slot_ref, f32[9216,128]{1,0:T(8,128)} %bitcast.9, f32[384,32,128]{2,1,0:T(8,128)} %bitcast.14, f32[8,128]{1,0:T(8,128)S(1)} %get-tuple-element.7.inv_ref), custom_call_target="tpu_custom_call" | custom-call | tf_op jit(solution)/shard_map/second_products/pallas_call | solution.py:406
  109.6 72.8 %col_reduce.1 = f32[64,3072]{1,0:T(8,128)S(1)} custom-call(f32[4,64,3072]{2,1,0:T(8,128)S(1)} %second_products.1.p_ref), custom_call_target="tpu_custom_call" | custom-call | tf_op jit(solution)/shard_map/col_reduce/pallas_call | solution.py:415
  182.4 0.9 copy.8
  183.2 0.9 copy.9
Async XLA Ops:
  0.6 18.1 %copy-start.1 = (f32[128,128]{1,0:T(8,128)S(1)}, f32[128,128]{1,0:T(8,128)}, u32[]{:S(2)}) copy-start(f32[128,128]{1,0:T(8,128)} %constant.2.clone.had_ref) | copy-start | bytes 196612
  10.3 2.3 %copy-start = (f32[1,1,288,4096]{3,2,1,0:T(8,128)S(1)}, f32[1,1,288,4096]{3,2,1,0:T(8,128)}, u32[]{:S(2)}) copy-start(f32[1,1,288,4096]{3,2,1,0:T(8,128)} %param.4) | copy-start | bytes 14155780
